TPU v7x, 32 devices: a whole 2x2x4 slice. The times are simulated.
32 devices in a mesh: chan: 16 (over z, x, core), win: 2 (over y).
Axes of the slice: x: 2, y: 2, z: 4, core: 2. Of those that a mesh axis runs over, the one named last changes fastest.
Arguments:
- strain_rate: bfloat16 [2, 1024, 8192], P('win', 'chan'), may hold values from -600 to 600
- bandpass_taps: bfloat16 [65], replicated, may hold values from -0.75 to 0.75
- pair_offsets: int32 [16, 6], P('chan'), may hold values from -1 to 15, as said below
- lag_limit: int32 [16, 6], P('chan'), may hold values from 1 to 8
Outputs:
- correlations: float32 [6, 8192, 2176], P(None, ('chan', 'win'))
Inputs may be any that keep to these rules, and one draw needn't show every extreme that they name: `pair_offsets`: row b lists distinct block offsets o (partner block (b + o) mod 16) in its first slots and -1 in the remaining slots; every row has at least one offset, some row uses all 6 slots and some row only one.
All inputs are finite; a program needn't handle non-finite values.
Results may differ from a plain program's by a relative error of at most 0.0027.
Values may be sent and summed in bfloat16 or wider, within the bound.
A program may use at most 128 MiB of HBM per device.

v0:
```python
import math

import jax
import jax.numpy as jnp
from jax import lax
from jax.sharding import PartitionSpec as P

VIRTUAL_SOURCES = 128
MAXIMUM_LAG = 8


def shifted(block, axis, distance):
    devices = range(lax.axis_size(axis))
    route = [((i - distance) % len(devices), i) for i in devices]
    return lax.ppermute(block, axis, route)


def band_filter(values, taps):
    samples, channel_count = values.shape
    tap_count = taps.shape[0]
    half_width = (tap_count - 1) // 2
    block_len = min(256, samples)
    pieces = samples // block_len
    padded = jnp.pad(values, ((half_width, half_width), (0, 0)))
    head_rows = padded[:samples].reshape(pieces, block_len, channel_count)
    rest_rows = jnp.pad(padded[block_len:], ((0, block_len - 2 * half_width), (0, 0)))
    tail_rows = rest_rows.reshape(pieces, block_len, channel_count)[:, : 2 * half_width]
    window = jnp.concatenate([head_rows, tail_rows], axis=1)
    period = jnp.concatenate([taps, jnp.zeros((block_len,), taps.dtype)])
    matrix = jnp.tile(period, block_len)[: block_len * (block_len + 2 * half_width)]
    matrix = matrix.reshape(block_len, block_len + 2 * half_width)
    filtered = jnp.einsum("ij,bjc->bic", matrix, window, preferred_element_type=jnp.float32)
    return filtered.reshape(samples, channel_count)


def normalize(window, taps):
    filtered = band_filter(window, taps)
    tap_count = taps.shape[0]
    magnitude = jnp.abs(filtered).astype(jnp.bfloat16)
    box_taps = jnp.ones((tap_count,), jnp.bfloat16)
    mean_level = band_filter(magnitude, box_taps) * (1.0 / tap_count)
    return (filtered / (mean_level + 1e-05)).astype(jnp.bfloat16)


def prepare(windows, taps):
    return jax.vmap(lambda window: normalize(window, taps))(windows)


def lagged(source_traces):
    samples = source_traces.shape[1]
    padded = jnp.pad(source_traces, ((0, 0), (MAXIMUM_LAG, MAXIMUM_LAG)))
    lag_rows = [
        padded[:, lag_index : lag_index + samples] for lag_index in range(2 * MAXIMUM_LAG + 1)
    ]
    return jnp.concatenate(lag_rows, axis=0)


def correlate(receivers, source_traces):
    stacked = lagged(source_traces)
    return lax.dot_general(
        receivers, stacked, (((0,), (1,)), ((), ())), preferred_element_type=jnp.float32
    )


def accumulate(totals, receivers, source_traces, offset_now, offsets, lag_mask):
    matched = offsets == offset_now

    def include(current):
        product = correlate(receivers, source_traces)
        weights = lag_mask * matched.astype(jnp.float32)[:, None]
        return current + weights[:, None, :] * product[None]

    return lax.cond(jnp.any(matched), include, lambda current: current, totals)


def on_device(strain_rate, bandpass_taps, pair_offsets, lag_limit):
    cleaned = (lambda windows: prepare(windows, bandpass_taps))(
        lax.all_to_all(strain_rate, "chan", split_axis=2, concat_axis=1, tiled=True)
    )
    receivers = cleaned[0]
    samples, channel_count = receivers.shape
    source_spacing = channel_count // VIRTUAL_SOURCES
    source_traces = jnp.transpose(receivers[:, ::source_spacing])
    offsets = pair_offsets[0]
    limits = lag_limit[0]
    column_list = (2 * MAXIMUM_LAG + 1) * VIRTUAL_SOURCES
    lag_samples = jnp.arange(column_list, dtype=jnp.int32) // VIRTUAL_SOURCES - MAXIMUM_LAG
    valid = (offsets >= 0)[:, None]
    lag_mask = ((jnp.abs(lag_samples)[None, :] <= limits[:, None]) & valid).astype(jnp.float32)
    blocks = lax.axis_size("chan")
    totals = jnp.zeros((offsets.shape[0], channel_count, column_list), jnp.float32)
    totals = accumulate(totals, receivers, source_traces, 0, offsets, lag_mask)

    def advance(step_index, state_now):
        current, held_panel = state_now
        held_panel = shifted(held_panel, "chan", -1)
        current = accumulate(current, receivers, held_panel, step_index, offsets, lag_mask)
        return (current, held_panel)

    totals, unused_panel = lax.fori_loop(1, blocks, advance, (totals, source_traces))
    summed = lax.psum_scatter(totals, "win", scatter_dimension=1, tiled=True)
    factor = 1.0 / math.sqrt(samples * lax.axis_size("win"))
    return summed * factor


def solution(mesh):
    placed = (P("win", "chan", None), P(), P("chan", None), P("chan", None))
    return jax.shard_map(
        on_device,
        mesh=mesh,
        in_specs=placed,
        out_specs=P(None, ("chan", "win"), None),
        check_vma=False,
    )
```

profile of v0, /device:TPU:3, one launch (start us, length us, event | category | flops | bytes accessed | tf_op | source)
XLA Modules:
  0.0 908.9 jit_solution(7040270174222355369)
XLA Ops:
  6.5 9.2 %copy.35 = bf16[1,64,8192]{1,0,2:T(2,128)(2,1)} copy(bf16[1,64,8192]{2,1,0:T(8,128)(2,1)} %param.10) | data formatting | bytes 2097152 | tf_op args[0]
  16.3 45.3 %reduce = bf16[8192,64]{1,0:T(8,128)(2,1)S(1)} reduce(bf16[8192,1,64]{2,1,0:T(2,128)(2,1)} %bitcast.56, bf16[]{:T(256)} %broadcast.93), dimensions={1}, to_apply=%bitcast.45.reduce_sub_computation | reduce | bytes 2097154
  61.6 2.2 reshape.108
  63.8 6.7 all-to-all-start
  72.3 0.7 broadcast_compare_fusion.1
  73.8 20.2 %all-to-all-done = bf16[16,2,16384]{2,1,0:T(2,128)(2,1)S(1)} async-done(((bf16[16,2,16384]{2,1,0:T(2,128)(2,1)}), bf16[16,2,16384]{2,1,0:T(2,128)(2,1)S(1)}, u32[]{:S(2)}, u32[]{:S(2)}) %all-to-all-start) | async-done | bytes 1048608 | tf_op jit(solution)/shard_map/all_to_all | solution.py:78
  94.0 7.0 reshape.109
  100.9 8.2 copy.36
  110.3 0.7 fusion.18
  111.3 0.8 divide_convert_fusion
  112.1 10.4 %slice.133 = bf16[1024,128]{1,0:T(8,128)(2,1)S(1)} slice(bf16[1024,512]{1,0:T(8,128)(2,1)S(1)} %bitcast.70), slice={[0:1024:1], [0:512:4]} | slice | bytes 524288 | tf_op jit(solution)/shard_map/slice | solution.py:83
  122.6 10.6 %conditional.2 = (f32[6,512,2176]{2,1,0:T(8,128)}) conditional(s32[]{:T(128)} %convert_element_type.47, () %tuple.35, (pred[6]{0:T(512)(128)(4,1)S(1)}, f32[6,2176]{1,0:T(8,128)S(1)}, bf16[128,1024]{0,1:T(8,128)(2,1)S(1)}, bf16[1024,512]{1,0:T(8,128)(2,1)S(1)}) %tuple.78), branch_computations={%region_1.2_spmd, %region_2.3_spmd} | conditional | flops 2288399104 | bytes 59663424 | solution.py:73
  122.6 10.5 %broadcast_in_dim.0 = f32[6,512,2176]{2,1,0:T(8,128)} broadcast(f32[]{:T(128)} %constant.44.clone), dimensions={} | broadcast | bytes 26738692 | tf_op jit(solution)/shard_map/broadcast_in_dim | solution.py:91
  133.2 397.1 %while.19 = (s32[]{:T(128)}, f32[6,512,2176]{2,1,0:T(8,128)}, bf16[128,1024]{1,0:T(8,128)(2,1)S(1)}, s32[6]{0:T(128)S(1)}, bf16[1024,512]{1,0:T(8,128)(2,1)S(1)}...) while((s32[]{:T(128)}, f32[6,512,2176]{2,1,0:T(8,128)}, ...), condition=%wide.region_7.8_spmd.clone, body=%wide.region_3.7_spmd.clone.sunk | while | flops 2295122944 | bytes 87511856 | solution.py:100
  133.2 0.6 fusion.24
  134.5 5.3 collective-permute-done
  139.8 35.2 %conditional.5 = (f32[6,512,2176]{2,1,0:T(8,128)}) conditional(s32[]{:T(128)} %convert_element_type.61, f32[6,512,2176]{2,1,0:T(8,128)} %get-tuple-element.320, (pred[6]{0:T(512)(128)(4,1)S(1)}, f32[6,2176]{1,0:T(8,128)S(1)}, bf16[128,1024]{1,0:T(8,128)(2,1)S(1)}, bf16[1024,512]{1,0:T(8,128)(2,1)S(1)}, f32[6,512,2176]{2,1,0:T(8,128)}) %tuple.67), branch_computations={%region_5.5_spmd, %region_6.6_spmd} | conditional | flops 2295083776 | bytes 85877824 | solution.py:73
  142.2 4.7 convolution_bitcast_fusion.1
  146.8 5.8 copy.34
  152.7 22.4 %multiply_add_fusion = f32[6,512,2176]{2,1,0:T(8,128)} fusion(f32[6,512,2176]{2,1,0:T(8,128)} %get-tuple-element.139, f32[512,2176]{1,0:T(8,128)} %copy.34, f32[6,2176]{1,0:T(8,128)S(1)} %broadcast_multiply_fusion.2), kind=kLoop, calls=%fused_computation.21 | loop fusion | flops 13369344 | bytes 57986048 | tf_op jit(solution)/shard_map/while/body/eval_jaxpr/cond/branch_1_fun/add | solution.py:71
  175.2 0.6 fusion.24
  176.5 5.3 collective-permute-done
  182.0 0.6 fusion.24
  183.3 5.3 collective-permute-done
  188.8 0.6 fusion.24
  190.1 5.3 collective-permute-done
  195.4 31.6 %collective-permute-start = (bf16[128,1024]{1,0:T(8,128)(2,1)S(1)}, bf16[128,1024]{1,0:T(8,128)(2,1)S(1)}, u32[]{:S(2)}, u32[]{:S(2)}) collective-permute-start(bf16[128,1024]{1,0:T(8,128)(2,1)S(1)} %get-tuple-element.321), channel_id=1, source_target_pairs={{2,0},{4,2},{6,4},{8,6},{10,8},{12,10},{14,12},{16,14},{18,16},{20... | collective-permute-start | bytes 786440 | tf_op jit(solution)/shard_map/while/body/eval_jaxpr/ppermute | solution.py:15
  228.5 72.9 %collective-permute-start = (bf16[128,1024]{1,0:T(8,128)(2,1)S(1)}, bf16[128,1024]{1,0:T(8,128)(2,1)S(1)}, u32[]{:S(2)}, u32[]{:S(2)}) collective-permute-start(bf16[128,1024]{1,0:T(8,128)(2,1)S(1)} %get-tuple-element.321), channel_id=1, source_target_pairs={{2,0},{4,2},{6,4},{8,6},{10,8},{12,10},{14,12},{16,14},{18,16},{20... | collective-permute-start | bytes 786440 | tf_op jit(solution)/shard_map/while/body/eval_jaxpr/ppermute | solution.py:15
  301.5 0.6 fusion.24
  302.9 2.5 collective-permute-start
  306.8 2.8 collective-permute-done
  309.6 36.8 %collective-permute-start = (bf16[128,1024]{1,0:T(8,128)(2,1)S(1)}, bf16[128,1024]{1,0:T(8,128)(2,1)S(1)}, u32[]{:S(2)}, u32[]{:S(2)}) collective-permute-start(bf16[128,1024]{1,0:T(8,128)(2,1)S(1)} %get-tuple-element.321), channel_id=1, source_target_pairs={{2,0},{4,2},{6,4},{8,6},{10,8},{12,10},{14,12},{16,14},{18,16},{20... | collective-permute-start | bytes 786440 | tf_op jit(solution)/shard_map/while/body/eval_jaxpr/ppermute | solution.py:15
  346.6 0.6 fusion.24
  347.9 4.4 collective-permute-start
  352.4 0.6 fusion.24
  353.7 0.9 collective-permute-done
  354.7 35.2 %conditional.5 = (f32[6,512,2176]{2,1,0:T(8,128)}) conditional(s32[]{:T(128)} %convert_element_type.61, f32[6,512,2176]{2,1,0:T(8,128)} %get-tuple-element.320, (pred[6]{0:T(512)(128)(4,1)S(1)}, f32[6,2176]{1,0:T(8,128)S(1)}, bf16[128,1024]{1,0:T(8,128)(2,1)S(1)}, bf16[1024,512]{1,0:T(8,128)(2,1)S(1)}, f32[6,512,2176]{2,1,0:T(8,128)}) %tuple.67), branch_computations={%region_5.5_spmd, %region_6.6_spmd} | conditional | flops 2295083776 | bytes 85877824 | solution.py:73
  357.0 4.7 convolution_bitcast_fusion.1
  361.7 5.8 copy.34
  367.5 22.4 %multiply_add_fusion = f32[6,512,2176]{2,1,0:T(8,128)} fusion(f32[6,512,2176]{2,1,0:T(8,128)} %get-tuple-element.139, f32[512,2176]{1,0:T(8,128)} %copy.34, f32[6,2176]{1,0:T(8,128)S(1)} %broadcast_multiply_fusion.2), kind=kLoop, calls=%fused_computation.21 | loop fusion | flops 13369344 | bytes 57986048 | tf_op jit(solution)/shard_map/while/body/eval_jaxpr/cond/branch_1_fun/add | solution.py:71
  391.3 7.8 collective-permute-done
  400.6 37.7 %collective-permute-done = bf16[128,1024]{1,0:T(8,128)(2,1)S(1)} collective-permute-done((bf16[128,1024]{1,0:T(8,128)(2,1)S(1)}, bf16[128,1024]{1,0:T(8,128)(2,1)S(1)}, u32[]{:S(2)}, u32[]{:S(2)}) %collective-permute-start) | collective-permute-done | bytes 262176 | tf_op jit(solution)/shard_map/while/body/eval_jaxpr/ppermute | solution.py:15
  439.8 37.7 %collective-permute-done = bf16[128,1024]{1,0:T(8,128)(2,1)S(1)} collective-permute-done((bf16[128,1024]{1,0:T(8,128)(2,1)S(1)}, bf16[128,1024]{1,0:T(8,128)(2,1)S(1)}, u32[]{:S(2)}, u32[]{:S(2)}) %collective-permute-start) | collective-permute-done | bytes 262176 | tf_op jit(solution)/shard_map/while/body/eval_jaxpr/ppermute | solution.py:15
  479.0 37.7 %collective-permute-done = bf16[128,1024]{1,0:T(8,128)(2,1)S(1)} collective-permute-done((bf16[128,1024]{1,0:T(8,128)(2,1)S(1)}, bf16[128,1024]{1,0:T(8,128)(2,1)S(1)}, u32[]{:S(2)}, u32[]{:S(2)}) %collective-permute-start) | collective-permute-done | bytes 262176 | tf_op jit(solution)/shard_map/while/body/eval_jaxpr/ppermute | solution.py:15
  518.2 5.3 collective-permute-done
  524.9 5.3 collective-permute-done
  530.3 360.8 %reduce-scatter.2.cloned.1.call-done = f32[6,256,2176]{2,1,0:T(8,128)} async-done(((f32[6,512,2176]{2,1,0:T(8,128)}), f32[6,256,2176]{2,1,0:T(8,128)}) %reduce-scatter.2.cloned.1.call-update) | async-done | bytes 13369360 | tf_op jit(solution)/shard_map/reduce_scatter | solution.py:101
  891.1 11.0 %broadcast_multiply_fusion.3 = f32[6,256,2176]{2,1,0:T(8,128)} fusion(f32[6,256,2176]{2,1,0:T(8,128)} %reduce-scatter.2.cloned.1.call-done), kind=kLoop, calls=%fused_computation.43 | loop fusion | flops 3342336 | bytes 26738688 | tf_op jit(solution)/shard_map/mul | solution.py:103
  (136 shorter events, 15.7 us)
Async XLA Ops:
  16.3 54.5 %copy-start.3 = (bf16[65]{0:T(256)(128)(2,1)S(1)}, bf16[65]{0:T(256)(128)(2,1)}, u32[]{:S(2)}) copy-start(bf16[65]{0:T(256)(128)(2,1)} %param.11) | copy-start | bytes 394
  61.6 9.9 %copy-start.2 = (bf16[321]{0:T(512)(128)(2,1)S(1)}, bf16[321]{0:T(512)(128)(2,1)}, u32[]{:S(2)}) copy-start(bf16[321]{0:T(512)(128)(2,1)} %constant.53.clone.1) | copy-start | bytes 1930
  61.6 10.7 %copy-start = (s32[1,6]{1,0:T(1,128)S(1)}, s32[1,6]{1,0:T(1,128)}, u32[]{:S(2)}) copy-start(s32[1,6]{1,0:T(1,128)} %param.12) | copy-start | bytes 76
  61.6 12.1 %copy-start.1 = (s32[1,6]{1,0:T(1,128)S(1)}, s32[1,6]{1,0:T(1,128)}, u32[]{:S(2)}) copy-start(s32[1,6]{1,0:T(1,128)} %param.13) | copy-start | bytes 76
  63.8 30.1 %all-to-all-start = ((bf16[16,2,16384]{2,1,0:T(2,128)(2,1)}), bf16[16,2,16384]{2,1,0:T(2,128)(2,1)S(1)}, u32[]{:S(2)}, u32[]{:S(2)}) async-start(bf16[16,2,16384]{2,1,0:T(2,128)(2,1)} %reshape.108), calls=%async_computation | async-start | bytes 2097152 | tf_op jit(solution)/shard_map/all_to_all | solution.py:78
  70.5 820.6 %reduce-scatter.2.cloned.1.call-start = ((), (), s32[]{:S(2)}) async-start(), calls=%async_computation.2 | async-start | bytes 40108032 | tf_op jit(solution)/shard_map/reduce_scatter | solution.py:101
  133.2 6.7 collective-permute-start
  175.1 6.7 collective-permute-start
  181.9 6.7 collective-permute-start
  188.6 6.7 collective-permute-start
  195.4 33.0 %collective-permute-start = (bf16[128,1024]{1,0:T(8,128)(2,1)S(1)}, bf16[128,1024]{1,0:T(8,128)(2,1)S(1)}, u32[]{:S(2)}, u32[]{:S(2)}) collective-permute-start(bf16[128,1024]{1,0:T(8,128)(2,1)S(1)} %get-tuple-element.321), channel_id=1, source_target_pairs={{2,0},{4,2},{6,4},{8,6},{10,8},{12,10},{14,12},{16,14},{18,16},{20... | collective-permute-start | bytes 786440 | tf_op jit(solution)/shard_map/while/body/eval_jaxpr/ppermute | solution.py:15
  228.5 74.3 %collective-permute-start = (bf16[128,1024]{1,0:T(8,128)(2,1)S(1)}, bf16[128,1024]{1,0:T(8,128)(2,1)S(1)}, u32[]{:S(2)}, u32[]{:S(2)}) collective-permute-start(bf16[128,1024]{1,0:T(8,128)(2,1)S(1)} %get-tuple-element.321), channel_id=1, source_target_pairs={{2,0},{4,2},{6,4},{8,6},{10,8},{12,10},{14,12},{16,14},{18,16},{20... | collective-permute-start | bytes 786440 | tf_op jit(solution)/shard_map/while/body/eval_jaxpr/ppermute | solution.py:15
  302.9 6.7 collective-permute-start
  309.6 38.2 %collective-permute-start = (bf16[128,1024]{1,0:T(8,128)(2,1)S(1)}, bf16[128,1024]{1,0:T(8,128)(2,1)S(1)}, u32[]{:S(2)}, u32[]{:S(2)}) collective-permute-start(bf16[128,1024]{1,0:T(8,128)(2,1)S(1)} %get-tuple-element.321), channel_id=1, source_target_pairs={{2,0},{4,2},{6,4},{8,6},{10,8},{12,10},{14,12},{16,14},{18,16},{20... | collective-permute-start | bytes 786440 | tf_op jit(solution)/shard_map/while/body/eval_jaxpr/ppermute | solution.py:15
  347.9 6.7 collective-permute-start
  389.9 9.3 %collective-permute-start = (bf16[128,1024]{1,0:T(8,128)(2,1)S(1)}, bf16[128,1024]{1,0:T(8,128)(2,1)S(1)}, u32[]{:S(2)}, u32[]{:S(2)}) collective-permute-start(bf16[128,1024]{1,0:T(8,128)(2,1)S(1)} %get-tuple-element.321), channel_id=1, source_target_pairs={{2,0},{4,2},{6,4},{8,6},{10,8},{12,10},{14,12},{16,14},{18,16},{20... | collective-permute-start | bytes 786440 | tf_op jit(solution)/shard_map/while/body/eval_jaxpr/ppermute | solution.py:15
  399.2 39.1 %collective-permute-start = (bf16[128,1024]{1,0:T(8,128)(2,1)S(1)}, bf16[128,1024]{1,0:T(8,128)(2,1)S(1)}, u32[]{:S(2)}, u32[]{:S(2)}) collective-permute-start(bf16[128,1024]{1,0:T(8,128)(2,1)S(1)} %get-tuple-element.321), channel_id=1, source_target_pairs={{2,0},{4,2},{6,4},{8,6},{10,8},{12,10},{14,12},{16,14},{18,16},{20... | collective-permute-start | bytes 786440 | tf_op jit(solution)/shard_map/while/body/eval_jaxpr/ppermute | solution.py:15
  438.4 39.1 %collective-permute-start = (bf16[128,1024]{1,0:T(8,128)(2,1)S(1)}, bf16[128,1024]{1,0:T(8,128)(2,1)S(1)}, u32[]{:S(2)}, u32[]{:S(2)}) collective-permute-start(bf16[128,1024]{1,0:T(8,128)(2,1)S(1)} %get-tuple-element.321), channel_id=1, source_target_pairs={{2,0},{4,2},{6,4},{8,6},{10,8},{12,10},{14,12},{16,14},{18,16},{20... | collective-permute-start | bytes 786440 | tf_op jit(solution)/shard_map/while/body/eval_jaxpr/ppermute | solution.py:15
  477.5 39.1 %collective-permute-start = (bf16[128,1024]{1,0:T(8,128)(2,1)S(1)}, bf16[128,1024]{1,0:T(8,128)(2,1)S(1)}, u32[]{:S(2)}, u32[]{:S(2)}) collective-permute-start(bf16[128,1024]{1,0:T(8,128)(2,1)S(1)} %get-tuple-element.321), channel_id=1, source_target_pairs={{2,0},{4,2},{6,4},{8,6},{10,8},{12,10},{14,12},{16,14},{18,16},{20... | collective-permute-start | bytes 786440 | tf_op jit(solution)/shard_map/while/body/eval_jaxpr/ppermute | solution.py:15
  516.7 6.7 collective-permute-start
  523.5 6.7 collective-permute-start
Sparse Core Ops, SparseCore 0:
  530.4 360.5 reduce-scatter.1
where the time goes:
time: 917 us; the launch traced here: 909 us
  waiting for transfers between devices  537 us (59%)
  starting transfers between devices  156 us (17%)
  other arithmetic  113 us (12%)
  local copies, waits for them, and re-layouts  67.3 us (7%)
  between operations  14.4 us (2%)
  matrix products  10.8 us (1%)
  loops' own time  10.6 us (1%)
    reduce_scatter x1, waiting for transfers between devices, on_device(): summed = lax.psum_scatter(totals, 'win', scatter_dimension=1, tiled=True)  361 us
    ppermute x15, waiting for transfers between devices, shifted(): return lax.ppermute(block, axis, route)  157 us
    ppermute x15, starting transfers between devices, shifted(): return lax.ppermute(block, axis, route)  149 us
    unnamed x1, other arithmetic  45.3 us
    add x2, other arithmetic, include(): return current + weights[:, None, :] * product[None]  44.7 us
    all_to_all x1, waiting for transfers between devices, on_device(): lax.all_to_all(strain_rate, 'chan', split_axis=2, concat_axis=1, tiled=True)  20.2 us
    unnamed x14, local copies, waits for them, and re-layouts  19.5 us
  transfers between devices with their start and end apart: 17, of which 14 were waited for; matrix products, arithmetic and copies ran while one was open for 1% of the time, Pallas kernels for 0%

commit v1 on v0

v1 whole, which is shorter than its diff:
```python
import functools
import math

import jax
import jax.numpy as jnp
from jax import lax
from jax.experimental import pallas as pl
from jax.experimental.pallas import tpu as pltpu
from jax.sharding import PartitionSpec as P

VIRTUAL_SOURCES = 128
MAXIMUM_LAG = 8
LAGS = 2 * MAXIMUM_LAG + 1
PIECE = 256
REACH = 384
VMEM_LIMIT = 48 * 1024 * 1024


def band(row, half):
    wide = jnp.broadcast_to(row, (PIECE, REACH))
    return pltpu.roll(wide, 0, 1, stride=1, stride_axis=0).astype(jnp.bfloat16)


def normalize_kernel(half, taps_ref, x_ref, out_ref, src_ref, padded, level, filtered):
    parts, _, rows, channels = x_ref.shape
    samples = parts * rows
    tap_count = 2 * half + 1
    tail = padded.shape[0] - samples - half
    padded[:half] = jnp.zeros((half, channels), jnp.bfloat16)
    padded[half + samples :] = jnp.zeros((tail, channels), jnp.bfloat16)
    level[:half] = jnp.zeros((half, channels), jnp.bfloat16)
    level[half + samples :] = jnp.zeros((tail, channels), jnp.bfloat16)
    for i in range(parts):
        padded[half + i * rows : half + (i + 1) * rows] = x_ref[i, 0]
    taps = band(taps_ref[...], half)
    ones = jnp.where(
        lax.broadcasted_iota(jnp.int32, (1, REACH), 1) < tap_count, 1.0, 0.0
    ).astype(jnp.float32)
    box = band(ones, half)
    for p in range(samples // PIECE):
        low = p * PIECE
        value = jnp.dot(taps, padded[low : low + REACH], preferred_element_type=jnp.float32)
        filtered[low : low + PIECE] = value
        level[half + low : half + low + PIECE] = jnp.abs(value).astype(jnp.bfloat16)
    per = src_ref.shape[0]
    spacing = channels // per
    pick = (
        lax.broadcasted_iota(jnp.int32, (per, channels), 1)
        == spacing * lax.broadcasted_iota(jnp.int32, (per, channels), 0)
    )
    pick = jnp.where(pick, 1.0, 0.0).astype(jnp.bfloat16)
    for p in range(samples // PIECE):
        low = p * PIECE
        total = jnp.dot(box, level[low : low + REACH], preferred_element_type=jnp.float32)
        mean = total * (1.0 / tap_count)
        value = filtered[low : low + PIECE] / (mean + 1e-05)
        turned = jnp.transpose(value).astype(jnp.bfloat16)
        out_ref[:, low : low + PIECE] = turned
        src_ref[:, low : low + PIECE] = jnp.dot(
            pick, turned, preferred_element_type=jnp.float32
        ).astype(jnp.bfloat16)


def normalize(parts, taps):
    blocks, windows, rows, channels = parts.shape
    samples = blocks * rows
    half = (taps.shape[0] - 1) // 2
    sources = VIRTUAL_SOURCES // windows
    row = jnp.pad(taps.astype(jnp.float32), (0, REACH - taps.shape[0]))[None]
    return pl.pallas_call(
        functools.partial(normalize_kernel, half),
        grid=(windows,),
        out_shape=(
            jax.ShapeDtypeStruct((channels, windows * samples), jnp.bfloat16),
            jax.ShapeDtypeStruct((sources, windows * samples), jnp.bfloat16),
        ),
        in_specs=[
            pl.BlockSpec((1, REACH), lambda w: (0, 0)),
            pl.BlockSpec((blocks, 1, rows, channels), lambda w: (0, w, 0, 0)),
        ],
        out_specs=(
            pl.BlockSpec((channels, samples), lambda w: (0, w)),
            pl.BlockSpec((sources, samples), lambda w: (0, w)),
        ),
        scratch_shapes=[
            pltpu.VMEM((samples + REACH - PIECE, channels), jnp.bfloat16),
            pltpu.VMEM((samples + REACH - PIECE, channels), jnp.bfloat16),
            pltpu.VMEM((samples, channels), jnp.float32),
        ],
        compiler_params=pltpu.CompilerParams(vmem_limit_bytes=VMEM_LIMIT),
        name="normalize",
    )(row, parts)


def shift_kernel(x_ref, out_ref):
    rows, samples = x_ref.shape
    value = x_ref[...].astype(jnp.float32)
    spot = lax.broadcasted_iota(jnp.int32, (rows, samples), 1)
    for index in range(LAGS):
        lag = index - MAXIMUM_LAG
        if lag == 0:
            moved = value
        else:
            moved = pltpu.roll(value, lag % samples, 1)
            kept = spot >= lag if lag > 0 else spot < samples + lag
            moved = jnp.where(kept, moved, 0.0)
        out_ref[index] = moved.astype(jnp.bfloat16)


def shift(receivers, windows):
    channels, length = receivers.shape
    samples = length // windows
    rows = min(32, channels)
    return pl.pallas_call(
        shift_kernel,
        grid=(channels // rows, windows),
        out_shape=jax.ShapeDtypeStruct((LAGS, channels, length), jnp.bfloat16),
        in_specs=[pl.BlockSpec((rows, samples), lambda c, w: (c, w))],
        out_specs=pl.BlockSpec((LAGS, rows, samples), lambda c, w: (0, c, w)),
        compiler_params=pltpu.CompilerParams(vmem_limit_bytes=VMEM_LIMIT),
        cost_estimate=pl.CostEstimate(
            flops=2 * LAGS * channels * length,
            bytes_accessed=2 * (LAGS + 1) * channels * length,
            transcendentals=0,
        ),
        name="shift",
    )(receivers)


def correlate_kernel(factor, partner, limit, lhs_ref, *refs):
    source_refs, out_ref = refs[:-1], refs[-1]
    slots = len(source_refs)
    lag = jnp.abs(pl.program_id(0) - MAXIMUM_LAG)
    for first in range(0, slots, 2):
        group = range(first, min(first + 2, slots))
        reach = functools.reduce(jnp.maximum, [limit[k] for k in group])

        @pl.when(lag <= reach)
        def _():
            panel = jnp.concatenate([source_refs[k][0] for k in group], axis=0)
            product = lax.dot_general(
                lhs_ref[0], panel, (((1,), (1,)), ((), ())), preferred_element_type=jnp.float32
            )
            for i, k in enumerate(group):
                piece = product[:, i * VIRTUAL_SOURCES : (i + 1) * VIRTUAL_SOURCES]
                out_ref[k] = jnp.where(lag <= limit[k], piece * factor, 0.0)

        @pl.when(lag > reach)
        def _():
            for k in group:
                out_ref[k] = jnp.zeros(out_ref.shape[1:], jnp.float32)


def correlate(lagged, gathered, partner, limit):
    _, channels, length = lagged.shape
    slots = partner.shape[0]

    def source_spec(k):
        return pl.BlockSpec(
            (1, VIRTUAL_SOURCES, length), lambda l, partner, limit: (partner[k], 0, 0)
        )

    return pl.pallas_call(
        functools.partial(correlate_kernel, 1.0 / math.sqrt(length)),
        grid_spec=pltpu.PrefetchScalarGridSpec(
            num_scalar_prefetch=2,
            grid=(LAGS,),
            in_specs=[pl.BlockSpec((1, channels, length), lambda l, partner, limit: (l, 0, 0))]
            + [source_spec(k) for k in range(slots)],
            out_specs=pl.BlockSpec(
                (slots, channels, VIRTUAL_SOURCES), lambda l, partner, limit: (0, 0, l)
            ),
        ),
        out_shape=jax.ShapeDtypeStruct((slots, channels, LAGS * VIRTUAL_SOURCES), jnp.float32),
        compiler_params=pltpu.CompilerParams(vmem_limit_bytes=VMEM_LIMIT),
        name="correlate",
    )(partner, limit, lagged, *[gathered] * slots)


def gather(sources, blocks):
    gathered = lax.all_gather(sources, ("chan", "win"))
    return gathered.reshape(blocks, VIRTUAL_SOURCES, sources.shape[1])


def gather_by_window(sources, partner, windows):
    samples = sources.shape[1] // windows
    blocks = lax.axis_size("chan")

    def one(window, panels):
        mine = lax.dynamic_slice_in_dim(sources, window * samples, samples, 1)
        mine = lax.all_gather(mine, "win", tiled=True)
        taken = lax.all_gather(mine, "chan")[partner]
        return lax.dynamic_update_slice_in_dim(panels, taken, window * samples, 2)

    empty = jnp.zeros((partner.shape[0], VIRTUAL_SOURCES, sources.shape[1]), sources.dtype)
    return lax.fori_loop(0, windows, one, empty)


def on_device(strain_rate, bandpass_taps, pair_offsets, lag_limit):
    blocks, windows = lax.axis_size("chan"), lax.axis_size("win")
    _, rows, total = strain_rate.shape
    channels = total // (blocks * windows)
    parts = lax.all_to_all(
        strain_rate[0], ("chan", "win"), split_axis=1, concat_axis=0, tiled=True
    ).reshape(blocks, windows, rows, channels)
    receivers, sources = normalize(parts, bandpass_taps)
    lagged = shift(receivers, windows)
    offsets = pair_offsets[0]
    used = offsets >= 0
    partner = jnp.where(used, (lax.axis_index("chan") + offsets) % blocks, 0).astype(jnp.int32)
    limit = jnp.where(used, lag_limit[0], -1).astype(jnp.int32)
    if windows > 2:
        panels = gather_by_window(sources, partner, windows)
        return correlate(lagged, panels, jnp.arange(partner.shape[0], dtype=jnp.int32), limit)
    return correlate(lagged, gather(sources, blocks), partner, limit)


def solution(mesh):
    placed = (P("win", "chan", None), P(), P("chan", None), P("chan", None))
    return jax.shard_map(
        on_device,
        mesh=mesh,
        in_specs=placed,
        out_specs=P(None, ("chan", "win"), None),
        check_vma=False,
    )
```

time: 917 us -> 159 us (0.17)
  the two profiles are of different devices: /device:TPU:3 before, /device:TPU:0 now
where the time goes in v1:
time: 159 us; the launch traced here: 158 us
  waiting for transfers between devices  90.2 us (57%)
  Pallas kernels  43.1 us (27%)
  between operations  13.4 us (8%)
  starting transfers between devices  7.34 us (5%)
  local copies, waits for them, and re-layouts  3.04 us (2%)
    all_gather x1, waiting for transfers between devices, gather(): gathered = lax.all_gather(sources, ('chan', 'win'))  64.7 us
    pallas_call x1, Pallas kernels, correlate(): pl.pallas_call(functools.partial(correlate_kernel, 1.0 / math.sqrt(length...  27.1 us
    all_to_all x1, waiting for transfers between devices, on_device(): lax.all_to_all(strain_rate[0], ('chan', 'win'), split_axis=1, concat_axis...  25.5 us
    pallas_call x1, Pallas kernels, shift(): pl.pallas_call(shift_kernel, grid=(channels // rows, windows), out_shape=...  11.2 us
    all_to_all x1, starting transfers between devices, on_device(): lax.all_to_all(strain_rate[0], ('chan', 'win'), split_axis=1, concat_axis...  7.3 us
    pallas_call x1, Pallas kernels, normalize(): pl.pallas_call(functools.partial(normalize_kernel, half), grid=(windows,)...  4.74 us
  transfers between devices with their start and end apart: 2, of which 2 were waited for; matrix products, arithmetic and copies ran while one was open for 1% of the time, Pallas kernels for 7%

profile of v1, /device:TPU:0, one launch (start us, length us, event | category | flops | bytes accessed | tf_op | source)
XLA Modules:
  0.0 158.5 jit_solution(3302125465280440656)
XLA Ops:
  6.5 1.5 copy.6
  8.0 1.6 copy.5
  9.6 7.3 %all-to-all-start = ((bf16[64,32,256]{2,0,1:T(8,128)(2,1)}), bf16[64,32,256]{2,0,1:T(8,128)(2,1)S(1)}, u32[]{:S(2)}, u32[]{:S(2)}) async-start(bf16[64,32,256]{2,0,1:T(8,128)(2,1)} %copy.5), calls=%async_computation | async-start | bytes 2097152 | tf_op jit(solution)/shard_map/all_to_all | solution.py:203
  16.9 0.0 all-gather.3.cloned.1.call-start
  16.9 0.7 pad_convert_fusion
  17.6 25.5 %all-to-all-done = bf16[64,32,256]{2,0,1:T(8,128)(2,1)S(1)} async-done(((bf16[64,32,256]{2,0,1:T(8,128)(2,1)}), bf16[64,32,256]{2,0,1:T(8,128)(2,1)S(1)}, u32[]{:S(2)}, u32[]{:S(2)}) %all-to-all-start) | async-done | bytes 1048608 | tf_op jit(solution)/shard_map/all_to_all | solution.py:203
  43.1 4.7 %normalize.1 = (bf16[256,2048]{1,0:T(8,128)(2,1)S(1)}, bf16[64,2048]{1,0:T(8,128)(2,1)}) custom-call(f32[1,384]{1,0:T(1,128)S(1)} %reshape.17.taps_ref, bf16[16,2,64,256]{3,2,1,0:T(8,128)(2,1)S(1)} %bitcast.14), custom_call_target="tpu_custom_call" | custom-call | tf_op jit(solution)/shard_map/normalize/pallas_call | solution.py:70
  47.9 0.0 all-gather.3.cloned.1.call-update
  47.9 0.7 bitcast_select_fusion
  48.6 11.2 %shift.1.lhs_ref = bf16[17,256,2048]{2,1,0:T(8,128)(2,1)} custom-call(bf16[256,2048]{1,0:T(8,128)(2,1)S(1)} %get-tuple-element.7.x_ref), custom_call_target="tpu_custom_call" | custom-call | flops 17825792 | bytes 18874368 | tf_op jit(solution)/shard_map/shift/pallas_call | solution.py:114
  59.8 64.7 %all-gather.3.cloned.1.call-done = bf16[2048,2048]{1,0:T(8,128)(2,1)} async-done(((bf16[64,2048]{1,0:T(8,128)(2,1)}), bf16[2048,2048]{1,0:T(8,128)(2,1)}) %all-gather.3.cloned.1.call-update) | async-done | bytes 8388624 | tf_op jit(solution)/shard_map/all_gather | solution.py:181
  124.5 27.1 %correlate.1 = f32[6,256,2176]{2,1,0:T(8,128)} custom-call(s32[6]{0:T(128)S(1)} %get-tuple-element.10.partner, s32[6]{0:T(128)S(1)} %get-tuple-element.9.limit, bf16[17,256,2048]{2,1,0:T(8,128)(2,1)} %shift.1.lhs_ref, bf16[16,128,2048]{2,1,0:T(8,128)(2,1)} %bitcast.15, bf16[16,128,2048]{2,1,0:T(8,128)(2,1)} %bitcast.16, bf16[16,128,2048]{2,1,0:T(8,128)(2,1)} %bitcast.17, ...), custom_call_target="tpu_custom_call" | custom-call | tf_op jit(solution)/shard_map/correlate/pallas_call | solution.py:163
  (1 shorter events, 0.0 us)
Async XLA Ops:
  9.6 33.5 %all-to-all-start = ((bf16[64,32,256]{2,0,1:T(8,128)(2,1)}), bf16[64,32,256]{2,0,1:T(8,128)(2,1)S(1)}, u32[]{:S(2)}, u32[]{:S(2)}) async-start(bf16[64,32,256]{2,0,1:T(8,128)(2,1)} %copy.5), calls=%async_computation | async-start | bytes 2097152 | tf_op jit(solution)/shard_map/all_to_all | solution.py:203
  16.9 107.6 %all-gather.3.cloned.1.call-start = ((), (), s32[]{:S(2)}) async-start(), calls=%async_computation.1 | async-start | bytes 8650752 | tf_op jit(solution)/shard_map/all_gather | solution.py:181
Sparse Core Ops, SparseCore 0:
  48.0 76.4 all-gather.2
